TPU v7x, 32 devices: a whole 2x2x4 slice. The times are simulated.
32 devices in a mesh: grp: 2 (over x), node: 8 (over z, y), tm: 2 (over core).
Axes of the slice: x: 2, y: 2, z: 4, core: 2. Of those that a mesh axis runs over, the one named last changes fastest.
Arguments:
- scaled_kelvin: float32 [128, 8192], P(('grp', 'node', 'tm')), parts along dimension 0, may hold values from 0.5 to 1.5
- surface_emittance: float32 [16384], P('grp'), parts along dimension 0, may hold values from 0.2 to 1
- loss_factors: float32 [128, 8192], P(('grp', 'node', 'tm')), parts along dimension 0, may hold values from -6 to 6
- gebhart_tiles: bfloat16 [128, 32, 128, 128], P(('grp', 'node')), parts along dimension 0, may hold values from 1.4603138e-06 to 0.0014648438
- tile_target_index: int32 [128, 32], P(('grp', 'node')), parts along dimension 0, may hold values from 0 to 63
- tile_slots_occupied: int32 [128], P(('grp', 'node')), parts along dimension 0, may hold values from 16 to 32, as said below
Outputs:
- temp_sensitivity: float32 [128, 8192], P(('grp', 'node', 'tm')), parts along dimension 0
There are 2 independent parts, one for each index of `grp`. A program takes and returns all parts, laid end to end along the dimension named above; each array names one. Nothing has to cross between parts.
Inputs may be any that keep to these rules, and one draw needn't show every extreme that they name: A row's slots k below tile_slots_occupied are used, the others are ignored; some row of every variant uses all 32.
All inputs are finite; a program needn't handle non-finite values.
Results may differ from a plain program's by a relative error of at most 0.0036.
Values may be sent and summed in bfloat16 or wider, within the bound.
A program may use at most 192 MiB of HBM per device.

v0:
```python
import jax
import jax.numpy as jnp
from jax import lax
from jax.sharding import PartitionSpec as P


def slot_window(gebhart_tiles, tile_target_index, tile_slots_occupied, slot_start, slot_width):
    in_use = (slot_start + jnp.arange(slot_width, dtype=jnp.int32))[None, :] < tile_slots_occupied[
        :, None
    ]
    return (gebhart_tiles, tile_target_index, in_use)


def over_slots(update, initial, slot_total):
    return update(initial, 0, slot_total)


def on_device(
    scaled_kelvin,
    surface_emittance,
    loss_factors,
    gebhart_tiles,
    tile_target_index,
    tile_slots_occupied,
):
    row_blocks, slot_total, block_side = (
        gebhart_tiles.shape[0],
        gebhart_tiles.shape[1],
        gebhart_tiles.shape[2],
    )
    surface_range = scaled_kelvin.shape[1]
    blocks_all = surface_range // block_side
    own_width = row_blocks * block_side
    own_start = lax.axis_index("node") * own_width
    radiant_output = (surface_emittance[None, :] * scaled_kelvin**4).astype(jnp.bfloat16)
    weights_here = lax.all_to_all(loss_factors, "node", split_axis=1, concat_axis=0, tiled=True)
    panel_rows = lax.all_gather(radiant_output, "node", axis=0, tiled=True)
    row_count = panel_rows.shape[0]
    panel_view = panel_rows.reshape(row_count, blocks_all, block_side)

    def update(running, slot_start, slot_width):
        tiles, columns, in_use = slot_window(
            gebhart_tiles, tile_target_index, tile_slots_occupied, slot_start, slot_width
        )
        picked = jnp.take(panel_view, columns.reshape(-1), axis=1)
        picked = picked.reshape(row_count, row_blocks, slot_width, block_side)
        picked = picked * in_use[None, :, :, None].astype(jnp.bfloat16)
        return jnp.einsum("nrkj,rkij->rni", picked, tiles, preferred_element_type=jnp.float32)

    flux = over_slots(
        update, jnp.zeros((row_blocks, row_count, block_side), jnp.float32), slot_total
    )
    flux = flux.transpose(1, 0, 2).reshape(row_count, own_width)
    own_emit = lax.dynamic_slice_in_dim(panel_rows, own_start, own_width, 1).astype(jnp.float32)
    weight_part = weights_here
    weight = weight_part * (flux - own_emit)
    sample_total = weight.shape[0]
    weight_rows = (
        weight.astype(jnp.bfloat16).reshape(sample_total, row_blocks, block_side).transpose(1, 0, 2)
    )
    weight_part = weight_rows

    def update(running, slot_start, slot_width):
        tiles, columns, in_use = slot_window(
            gebhart_tiles, tile_target_index, tile_slots_occupied, slot_start, slot_width
        )
        contrib = jnp.einsum(
            "rni,rkij->nrkj", weight_part, tiles, preferred_element_type=jnp.float32
        )
        targets = jnp.where(in_use, columns, blocks_all).reshape(-1)
        contrib = contrib.reshape(sample_total, row_blocks * slot_width, block_side)
        return running.at[:, targets, :].add(contrib, mode="drop")

    collected = over_slots(
        update, jnp.zeros((sample_total, blocks_all, block_side), jnp.float32), slot_total
    )
    summed = (
        lax.psum_scatter(
            collected.reshape(sample_total, surface_range).astype(jnp.bfloat16),
            "node",
            scatter_dimension=1,
            tiled=True,
        ).astype(jnp.float32)
        - weight
    )
    costate_vector = lax.all_to_all(summed, "node", split_axis=0, concat_axis=1, tiled=True)
    return 4.0 * surface_emittance[None, :] * scaled_kelvin**3 * costate_vector


def solution(mesh):
    placed = (
        P(("grp", "node", "tm"), None),
        P("grp"),
        P(("grp", "node", "tm"), None),
        P(("grp", "node"), None, None, None),
        P(("grp", "node"), None),
        P(("grp", "node")),
    )
    return jax.shard_map(
        on_device,
        mesh=mesh,
        in_specs=placed,
        out_specs=P(("grp", "node", "tm"), None),
        check_vma=False,
    )
```

profile of v0, /device:TPU:0, one launch (start us, length us, event | category | flops | bytes accessed | tf_op | source)
XLA Modules:
  0.0 169.4 jit_solution(2546197744501569730)
XLA Ops:
  6.5 7.3 %all-to-all-start = ((f32[4,8,1024]{2,0,1:T(4,128)}), f32[4,8,1024]{2,0,1:T(4,128)S(1)}, u32[]{:S(2)}, u32[]{:S(2)}) async-start(f32[4,8,1024]{2,0,1:T(4,128)} %bitcast.50), calls=%async_computation | async-start | bytes 262144 | tf_op jit(solution)/shard_map/all_to_all | solution.py:36
  13.8 0.0 reduce-scatter.2.cloned.1.call-start
  13.9 0.9 fusion.14
  14.8 31.9 %all-gather = bf16[8,4,8192]{2,1,0:T(4,128)(2,1)S(1)} all-gather(bf16[1,4,8192]{2,1,0:T(4,128)(2,1)S(1)} %fusion.14), channel_id=1, replica_groups=mesh['grp'=2,'node'=8,'tm'=2] {'node'}, dimensions={0}, use_global_device_ids=true | all-gather | bytes 589824 | tf_op jit(solution)/shard_map/all_gather | solution.py:37
  46.7 0.5 reshape.117
  47.3 0.3 copy.19
  47.6 0.8 reshape.118
  48.4 0.8 fusion.17
  49.2 1.0 gather_fusion
  50.2 0.0 copy-start.2
  50.2 0.0 copy-start.3
  50.2 5.2 %fusion.4 = f32[8,4,8,128]{3,2,1,0:T(8,128)S(1)} fusion(bf16[8,32,128,128]{3,2,1,0:T(8,128)(2,1)} %param.9, bf16[32,8,32,128]{3,0,2,1:T(8,128)(2,1)S(1)} %bitcast.46, pred[8,32]{1,0:T(8,128)(4,1)S(1)} %get-tuple-element.6, bf16[8,32]{1,0:T(8,128)(2,1)S(1)} %get-tuple-element.5), kind=kOutput, calls=%fused_computation.6 | convolution fusion | flops 270532608 | bytes 10617600 | tf_op jit(solution)/shard_map/nrkj,rkij->rni/dot_general | solution.py:48
  55.4 0.0 copy-done.2
  55.4 0.0 copy-done.3
  55.4 0.1 fusion.18
  55.5 0.1 reshape.139
  55.6 0.1 reshape.116
  55.7 0.0 all-to-all-done
  55.8 6.6 %fusion.15 = f32[8,32,32,128]{3,1,2,0:T(8,128)} fusion(bf16[8,32,128,128]{3,2,1,0:T(8,128)(2,1)} %param.9, bf16[8,32,128,1]{2,0,1,3:T(8,128)(2,1)S(1)} %bitcast.49), kind=kOutput, calls=%fused_computation.21 | convolution fusion | flops 268435456 | bytes 12648448 | tf_op jit(solution)/shard_map/rni,rkij->nrkj/dot_general | solution.py:67
  62.4 0.1 broadcast_in_dim.16
  62.5 0.0 copy-start.1
  62.5 0.0 copy-start
  62.5 22.5 %scatter_fusion = f32[32,64,128]{2,0,1:T(8,128)S(1)} fusion(f32[32,64,128]{2,0,1:T(8,128)S(1)} %broadcast_in_dim.16, s32[256]{0:T(256)S(1)} %bitcast.51, f32[256,32,128]{2,1,0:T(8,128)} %bitcast.45), kind=kCustom, calls=%fused_computation.1 | custom fusion | flops 1048576 | bytes 12583936 | tf_op jit(solution)/shard_map/scatter-add | solution.py:72
  85.1 0.8 copy_bitcast_fusion
  85.9 0.0 reduce-scatter.2.cloned.1.call-update
  86.0 63.4 %reduce-scatter.2.cloned.1.call-done = bf16[32,1024]{1,0:T(8,128)(2,1)} async-done(((bf16[32,8192]{1,0:T(8,128)(2,1)}), bf16[32,1024]{1,0:T(8,128)(2,1)}) %reduce-scatter.2.cloned.1.call-update) | async-done | bytes 65552 | tf_op jit(solution)/shard_map/reduce_scatter | solution.py:78
  149.3 0.9 convert_subtract_fusion
  150.2 0.7 all_to_all.32
  150.9 3.6 %all-to-all-start.1 = ((f32[8,4,1024]{2,1,0:T(4,128)}), f32[8,4,1024]{2,1,0:T(4,128)S(1)}, u32[]{:S(2)}, u32[]{:S(2)}) async-start(f32[8,4,1024]{2,1,0:T(4,128)} %all_to_all.32), calls=%async_computation.2 | async-start | bytes 262144 | tf_op jit(solution)/shard_map/all_to_all | solution.py:86
  154.5 0.0 copy-done.1
  154.5 7.3 %all-to-all-done.1 = f32[8,4,1024]{2,1,0:T(4,128)S(1)} async-done(((f32[8,4,1024]{2,1,0:T(4,128)}), f32[8,4,1024]{2,1,0:T(4,128)S(1)}, u32[]{:S(2)}, u32[]{:S(2)}) %all-to-all-start.1) | async-done | bytes 131104 | tf_op jit(solution)/shard_map/all_to_all | solution.py:86
  161.9 0.0 copy-done
  161.9 0.7 fusion.10
  (7 shorter events, 0.1 us)
Async XLA Ops:
  6.5 49.2 %all-to-all-start = ((f32[4,8,1024]{2,0,1:T(4,128)}), f32[4,8,1024]{2,0,1:T(4,128)S(1)}, u32[]{:S(2)}, u32[]{:S(2)}) async-start(f32[4,8,1024]{2,0,1:T(4,128)} %bitcast.50), calls=%async_computation | async-start | bytes 262144 | tf_op jit(solution)/shard_map/all_to_all | solution.py:36
  13.8 135.5 %reduce-scatter.2.cloned.1.call-start = ((), (), s32[]{:S(2)}) async-start(), calls=%async_computation.3 | async-start | bytes 589824 | tf_op jit(solution)/shard_map/reduce_scatter | solution.py:78
  50.2 5.2 %copy-start.2 = (s32[8,32]{1,0:T(8,128)S(1)}, s32[8,32]{1,0:T(8,128)}, u32[]{:S(2)}) copy-start(s32[8,32]{1,0:T(8,128)} %param.10) | copy-start | bytes 3076
  50.2 5.2 %copy-start.3 = (s32[8]{0:T(128)S(1)}, s32[8]{0:T(128)}, u32[]{:S(2)}) copy-start(s32[8]{0:T(128)} %param.11) | copy-start | bytes 100
  62.5 92.0 %copy-start.1 = (f32[8192]{0:T(1024)S(1)}, f32[8192]{0:T(1024)}, u32[]{:S(2)}) copy-start(f32[8192]{0:T(1024)} %param.7) | copy-start | bytes 98308
  62.5 99.3 %copy-start = (f32[4,8192]{1,0:T(4,128)S(1)}, f32[4,8192]{1,0:T(4,128)}, u32[]{:S(2)}) copy-start(f32[4,8192]{1,0:T(4,128)} %param.6) | copy-start | bytes 393220
  150.9 10.9 %all-to-all-start.1 = ((f32[8,4,1024]{2,1,0:T(4,128)}), f32[8,4,1024]{2,1,0:T(4,128)S(1)}, u32[]{:S(2)}, u32[]{:S(2)}) async-start(f32[8,4,1024]{2,1,0:T(4,128)} %all_to_all.32), calls=%async_computation.2 | async-start | bytes 262144 | tf_op jit(solution)/shard_map/all_to_all | solution.py:86
Sparse Core Ops, SparseCore 0:
  86.1 63.2 reduce-scatter.1
where the time goes:
time: 170 us; the launch traced here: 169 us
  waiting for transfers between devices  70.7 us (42%)
  blocking collectives  31.9 us (19%)
  other arithmetic  26.8 us (16%)
  between operations  13.5 us (8%)
  matrix products  11.7 us (7%)
  starting transfers between devices  10.9 us (6%)
  local copies, waits for them, and re-layouts  3.74 us (2%)
    reduce_scatter x1, waiting for transfers between devices, on_device(): lax.psum_scatter(collected.reshape(sample_total, surface_range).astype(jn...  63.4 us
    all_gather x1, blocking collectives, on_device(): panel_rows = lax.all_gather(radiant_output, 'node', axis=0, tiled=True)  31.9 us
    scatter-add x1, other arithmetic, update(): return running.at[:, targets, :].add(contrib, mode='drop')  22.5 us
    all_to_all x1, waiting for transfers between devices, on_device(): lax.all_to_all(summed, 'node', split_axis=0, concat_axis=1, tiled=True)  7.33 us
    all_to_all x1, starting transfers between devices, on_device(): lax.all_to_all(loss_factors, 'node', split_axis=1, concat_axis=0, tiled=T...  7.28 us
    dot_general x1, matrix products, update(): jnp.einsum('rni,rkij->nrkj', weight_part, tiles, preferred_element_type=j...  6.55 us
    dot_general x1, matrix products, update(): jnp.einsum('nrkj,rkij->rni', picked, tiles, preferred_element_type=jnp.fl...  5.19 us
    all_to_all x1, starting transfers between devices, on_device(): lax.all_to_all(summed, 'node', split_axis=0, concat_axis=1, tiled=True)  3.6 us
  transfers between devices with their start and end apart: 3, of which 2 were waited for; matrix products, arithmetic and copies ran while one was open for 6% of the time, Pallas kernels for 0%

commit v1 on v0

v1 whole, which is shorter than its diff:
```python
import functools

import jax
import jax.numpy as jnp
from jax import lax
from jax.experimental import pallas as pl
from jax.experimental.pallas import tpu as pltpu
from jax.sharding import PartitionSpec as P

MESH = pl.DeviceIdType.MESH
F32 = jnp.float32
BF16 = jnp.bfloat16
CHUNK = 16


def kernel(
    n,
    kelvin_ref,
    emit_ref,
    loss_ref,
    tiles_hbm,
    gather_ref,
    prev_ref,
    last_ref,
    out_ref,
    tiles,
    em_recv,
    em,
    loss_send,
    loss_recv,
    loss_rows,
    neg_weight,
    running,
    mix,
    stage,
    adj_recv,
    tile_sem,
    em_send_sem,
    em_recv_sem,
    loss_send_sem,
    loss_recv_sem,
    adj_send_sem,
    adj_recv_sem,
):
    me = lax.axis_index("node")
    rows, slots, side = tiles.shape[0], tiles.shape[1], tiles.shape[2]
    blocks = emit_ref.shape[0]
    tl = kelvin_ref.shape[0]
    samples = tl * n
    chunks = blocks // CHUNK
    ch_rows = CHUNK * tl
    entries = rows * slots

    def tile_copy(r):
        return pltpu.make_async_copy(tiles_hbm.at[r], tiles.at[r], tile_sem.at[r])

    for r in range(rows):
        tile_copy(r).start()

    barrier = pltpu.get_barrier_semaphore()
    for o in range(1, n):
        pl.semaphore_signal(
            barrier, inc=1, device_id={"node": lax.rem(me + o, n)}, device_id_type=MESH
        )

    def emit_chunk(ch, carry):
        first = pl.multiple_of(ch * ch_rows, ch_rows)
        for i in range(CHUNK):
            cols = pl.ds(pl.multiple_of((ch * CHUNK + i) * side, side), side)
            t2 = kelvin_ref[:, cols] * kelvin_ref[:, cols]
            stage[i * tl : (i + 1) * tl, :] = emit_ref[pl.ds(ch * CHUNK + i, 1), :] * (t2 * t2)
        em_recv[me, pl.ds(first, ch_rows), :] = stage[...].astype(BF16)
        for i in range(CHUNK):
            cols = pl.ds(pl.multiple_of((ch * CHUNK + i) * side, side), side)
            stage[i * tl : (i + 1) * tl, :] = loss_ref[:, cols]
        loss_send[pl.ds(first, ch_rows), :] = stage[...].astype(BF16)
        return carry

    lax.fori_loop(0, chunks, emit_chunk, 0)
    pl.semaphore_wait(barrier, n - 1)

    def em_copy(o, src, dst):
        return pltpu.make_async_remote_copy(
            src_ref=em_recv.at[src],
            dst_ref=em_recv.at[src],
            send_sem=em_send_sem.at[o],
            recv_sem=em_recv_sem.at[o],
            device_id={"node": dst},
            device_id_type=MESH,
        )

    def loss_copy(o, src, dst):
        part = pl.multiple_of(dst * (rows * tl), rows * tl)
        return pltpu.make_async_remote_copy(
            src_ref=loss_send.at[pl.ds(part, rows * tl)],
            dst_ref=loss_recv.at[src],
            send_sem=loss_send_sem.at[o],
            recv_sem=loss_recv_sem.at[o],
            device_id={"node": dst},
            device_id_type=MESH,
        )

    for o in range(1, n):
        em_copy(o, me, lax.rem(me + o, n)).start()
    for o in range(1, n):
        loss_copy(o, me, lax.rem(me + o, n)).start()

    em[blocks] = jnp.zeros((samples, side), BF16)
    neg_weight[rows] = jnp.zeros((samples, side), F32)
    running[entries] = jnp.zeros((samples, side), F32)
    own_part = pl.multiple_of(me * (rows * tl), rows * tl)
    loss_recv[me] = loss_send[pl.ds(own_part, rows * tl), :]

    for o in range(1, n):
        em_copy(o, lax.rem(me + n - o, n), lax.rem(me + o, n)).wait()

    def em_chunk(ch, carry):
        first = pl.multiple_of(ch * ch_rows, ch_rows)
        for s in range(n):
            mix[pl.ds(s, ch_rows, stride=n), :] = em_recv[s, pl.ds(first, ch_rows), :].astype(F32)
        for i in range(CHUNK):
            em[ch * CHUNK + i] = mix[i * samples : (i + 1) * samples, :].astype(BF16)
        return carry

    lax.fori_loop(0, chunks, em_chunk, 0)

    for o in range(1, n):
        loss_copy(o, lax.rem(me + n - o, n), lax.rem(me + o, n)).wait()
    for s in range(n):
        loss_rows[pl.ds(s, rows * tl, stride=n), :] = loss_recv[s].astype(F32)
    for r in range(rows):
        tile_copy(r).wait()

    def row_step(r, carry):
        flux = jnp.zeros((samples, side), F32)
        for k in range(slots):
            flux += lax.dot_general(
                em[gather_ref[r * slots + k]],
                tiles[r, k],
                (((1,), (1,)), ((), ())),
                preferred_element_type=F32,
            )
        own = em[me * rows + r].astype(F32)
        here = loss_rows[pl.ds(pl.multiple_of(r * samples, samples), samples), :]
        weight = here * (flux - own)
        neg_weight[r] = -weight
        weight_b = weight.astype(BF16)
        for k in range(slots):
            contrib = jnp.dot(weight_b, tiles[r, k], preferred_element_type=F32)
            running[r * slots + k] = contrib + running[prev_ref[r * slots + k]]
        return carry

    lax.fori_loop(0, rows, row_step, 0)

    def adj_copy(o, ch, src, dst):
        first = pl.multiple_of(ch * ch_rows, ch_rows)
        return pltpu.make_async_remote_copy(
            src_ref=em_recv.at[dst, pl.ds(first, ch_rows)],
            dst_ref=adj_recv.at[src, pl.ds(first, ch_rows)],
            send_sem=adj_send_sem.at[o, ch],
            recv_sem=adj_recv_sem.at[o, ch],
            device_id={"node": dst},
            device_id_type=MESH,
        )

    def send_chunk(ch, carry):
        first = pl.multiple_of(ch * ch_rows, ch_rows)
        for i in range(CHUNK):
            c = ch * CHUNK + i
            off = c - me * rows
            mine = jnp.where((off >= 0) & (off < rows), off, rows)
            mix[i * samples : (i + 1) * samples, :] = running[last_ref[c]] + neg_weight[mine]
        for s in range(n):
            em_recv[s, pl.ds(first, ch_rows), :] = mix[pl.ds(s, ch_rows, stride=n), :].astype(BF16)
        for o in range(1, n):
            adj_copy(o, ch, me, lax.rem(me + o, n)).start()
        return carry

    lax.fori_loop(0, chunks, send_chunk, 0)

    def sum_chunk(ch, carry):
        first = pl.multiple_of(ch * ch_rows, ch_rows)
        total = em_recv[me, pl.ds(first, ch_rows), :].astype(F32)
        for o in range(1, n):
            src = lax.rem(me + n - o, n)
            adj_copy(o, ch, src, lax.rem(me + o, n)).wait()
            total += adj_recv[src, pl.ds(first, ch_rows), :].astype(F32)
        stage[...] = total
        for i in range(CHUNK):
            cols = pl.ds(pl.multiple_of((ch * CHUNK + i) * side, side), side)
            out_ref[:, cols] = stage[i * tl : (i + 1) * tl, :]
        return carry

    lax.fori_loop(0, chunks, sum_chunk, 0)


def on_device(
    n,
    scaled_kelvin,
    surface_emittance,
    loss_factors,
    gebhart_tiles,
    tile_target_index,
    tile_slots_occupied,
):
    rows, slots, side = gebhart_tiles.shape[:3]
    tl, surfaces = scaled_kelvin.shape
    blocks = surfaces // side
    samples = tl * n
    entries = rows * slots

    in_use = jnp.arange(slots, dtype=jnp.int32)[None, :] < tile_slots_occupied[:, None]
    target = jnp.where(in_use, tile_target_index, blocks).reshape(entries)
    at = jnp.arange(entries, dtype=jnp.int32)
    same = (target[:, None] == target[None, :]) & (at[None, :] < at[:, None])
    prev = jnp.max(jnp.where(same, at[None, :], -1), axis=1)
    prev = jnp.where(prev < 0, entries, prev)
    hit = jnp.arange(blocks, dtype=jnp.int32)[:, None] == target[None, :]
    last = jnp.max(jnp.where(hit, at[None, :], -1), axis=1)
    last = jnp.where(last < 0, entries, last)

    vmem = pl.BlockSpec(memory_space=pltpu.VMEM)
    smem = pl.BlockSpec(memory_space=pltpu.SMEM)
    adjoint = pl.pallas_call(
        functools.partial(kernel, n),
        out_shape=jax.ShapeDtypeStruct((tl, surfaces), F32),
        in_specs=[vmem, vmem, vmem, pl.BlockSpec(memory_space=pl.ANY), smem, smem, smem],
        out_specs=vmem,
        scratch_shapes=[
            pltpu.VMEM(gebhart_tiles.shape, BF16),
            pltpu.VMEM((n, blocks * tl, side), BF16),
            pltpu.VMEM((blocks + 1, samples, side), BF16),
            pltpu.VMEM((blocks * tl, side), BF16),
            pltpu.VMEM((n, rows * tl, side), BF16),
            pltpu.VMEM((rows * samples, side), F32),
            pltpu.VMEM((rows + 1, samples, side), F32),
            pltpu.VMEM((entries + 1, samples, side), F32),
            pltpu.VMEM((CHUNK * samples, side), F32),
            pltpu.VMEM((CHUNK * tl, side), F32),
            pltpu.VMEM((n, blocks * tl, side), BF16),
            pltpu.SemaphoreType.DMA((rows,)),
            pltpu.SemaphoreType.DMA((n,)),
            pltpu.SemaphoreType.DMA((n,)),
            pltpu.SemaphoreType.DMA((n,)),
            pltpu.SemaphoreType.DMA((n,)),
            pltpu.SemaphoreType.DMA((n, blocks // CHUNK)),
            pltpu.SemaphoreType.DMA((n, blocks // CHUNK)),
        ],
        compiler_params=pltpu.CompilerParams(
            collective_id=0, has_side_effects=True, vmem_limit_bytes=60 * 2**20
        ),
    )(
        scaled_kelvin,
        surface_emittance.reshape(blocks, side),
        loss_factors,
        gebhart_tiles,
        target,
        prev,
        last,
    )
    return 4.0 * surface_emittance[None, :] * scaled_kelvin**3 * adjoint


def solution(mesh):
    placed = (
        P(("grp", "node", "tm"), None),
        P("grp"),
        P(("grp", "node", "tm"), None),
        P(("grp", "node"), None, None, None),
        P(("grp", "node"), None),
        P(("grp", "node")),
    )
    return jax.shard_map(
        functools.partial(on_device, mesh.shape["node"]),
        mesh=mesh,
        in_specs=placed,
        out_specs=P(("grp", "node", "tm"), None),
        check_vma=False,
    )
```

time: 170 us -> 51.4 us (0.30)
  waiting for transfers between devices: 70.7 us -> 0 us
  Pallas kernels: 0 us -> 47.3 us
  blocking collectives: 31.9 us -> 0 us
  other arithmetic: 26.8 us -> 3.88 us
  between operations: 13.5 us -> 0.04 us
  matrix products: 11.7 us -> 0 us
  starting transfers between devices: 10.9 us -> 0 us
  local copies, waits for them, and re-layouts: 3.74 us -> 0.09 us
    reduce_scatter x1 -> x0, waiting for transfers between devices: 63.4 us -> none  [on_device(): lax.psum_scatter(collected.reshape(sample_total, surface_range).astype(jn...]
    pallas_call x0 -> x1, Pallas kernels: none -> 47.3 us  [on_device(): pl.pallas_call(functools.partial(kernel, n), out_shape=jax.ShapeDtypeStru...]
    all_gather x1 -> x0, blocking collectives: 31.9 us -> none  [on_device(): panel_rows = lax.all_gather(radiant_output, 'node', axis=0, tiled=True)]
    scatter-add x1 -> x0, other arithmetic: 22.5 us -> none  [update(): return running.at[:, targets, :].add(contrib, mode='drop')]
    dot_general x2 -> x0, matrix products: 11.7 us -> none  [the longest x1 6.55 us: update(): jnp.einsum('rni,rkij->nrkj', weight_part, tiles, preferred_element_type=j...]
    all_to_all x2 -> x0, starting transfers between devices: 10.9 us -> none  [the longest x1 7.28 us: on_device(): lax.all_to_all(loss_factors, 'node', split_axis=1, concat_axis=0, tiled=T...]
    all_to_all x2 -> x0, waiting for transfers between devices: 7.33 us -> none  [the longest x1 7.33 us: on_device(): lax.all_to_all(summed, 'node', split_axis=0, concat_axis=1, tiled=True)]
    select_n x3, other arithmetic: 0.08 us -> 1.96 us  [the longest x1 0.79 us: on_device(): target = jnp.where(in_use, tile_target_index, blocks).reshape(entries)]
  transfers between devices with their start and end apart: 3 -> 0, of which waited for: 2 -> 0; matrix products, arithmetic and copies ran while one was open for 6% -> 0% of each run, Pallas kernels for 0% -> 0%
where the time goes in v1:
time: 51.4 us; the launch traced here: 51.3 us
  Pallas kernels  47.3 us (92%)
  other arithmetic  3.88 us (8%)
    pallas_call x1, Pallas kernels, on_device(): pl.pallas_call(functools.partial(kernel, n), out_shape=jax.ShapeDtypeStru...  47.3 us
    mul x2, other arithmetic, on_device(): return 4.0 * surface_emittance[None, :] * scaled_kelvin ** 3 * adjoint  1.62 us

profile of v1, /device:TPU:0, one launch (start us, length us, event | category | flops | bytes accessed | tf_op | source)
XLA Modules:
  0.0 51.3 jit_solution(1767408827680271495)
XLA Ops:
  0.0 0.0 copy-start.1
  0.0 0.0 copy-start
  0.0 0.8 %fusion.3 = s32[8,32]{1,0:T(8,128)S(1)} fusion(s32[8,32]{1,0:T(8,128)} %param.10, s32[8]{0:T(128)} %param.11), kind=kLoop, calls=%fused_computation.10 | loop fusion | flops 512 | bytes 2080 | tf_op jit(solution)/shard_map/jit(_where)/select_n | solution.py:213
  0.8 0.1 reshape.12.gather_ref
  0.9 0.0 copy-start.2
  0.9 0.2 select_reduce_fusion
  1.1 0.6 %compare_select_fusion.prev_ref = s32[256]{0:T(256)} fusion(s32[256]{0:T(256)S(1)} %select_reduce_fusion), kind=kLoop, calls=%fused_computation.11 | loop fusion | flops 512 | bytes 2048 | tf_op jit(solution)/shard_map/jit(_where)/select_n | solution.py:217
  1.6 0.1 select_reduce_fusion.1
  1.8 0.6 %compare_select_fusion.1.last_ref = s32[64]{0:T(128)} fusion(s32[64]{0:T(128)S(1)} %select_reduce_fusion.1), kind=kLoop, calls=%fused_computation.12 | loop fusion | flops 128 | bytes 512 | tf_op jit(solution)/shard_map/jit(_where)/select_n | solution.py:220
  2.4 0.0 copy-done.2
  2.4 47.3 %shard_map.64 = f32[4,8192]{1,0:T(4,128)} custom-call(f32[4,8192]{1,0:T(4,128)} %kelvin_ref.1, f32[64,128]{1,0:T(8,128)} %bitcast.1, f32[4,8192]{1,0:T(4,128)} %loss_ref.1, bf16[8,32,128,128]{3,2,1,0:T(8,128)(2,1)} %tiles_hbm.1, s32[256]{0:T(256)} %copy-done.2, s32[256]{0:T(256)} %compare_select_fusion.prev_ref, s32[64]{0:T(128)} %compare_select_fusion.1.last_ref), custom_call_target="tpu_custom_call" | custom-call | tf_op jit(solution)/shard_map/pallas_call | solution.py:224
  49.6 0.0 copy-done.1
  49.7 0.0 copy-done
  49.7 1.6 %fusion.2 = f32[4,8192]{1,0:T(4,128)} fusion(f32[4,8192]{1,0:T(4,128)} %shard_map.64, f32[4,8192]{1,0:T(4,128)S(1)} %copy-done, f32[8192]{0:T(1024)S(1)} %broadcast_multiply_fusion), kind=kLoop, calls=%fused_computation.5 | loop fusion | flops 131072 | bytes 425984 | tf_op jit(solution)/shard_map/mul | solution.py:261
  (1 shorter events, 0.0 us)
Async XLA Ops:
  0.0 49.6 %copy-start.1 = (f32[8192]{0:T(1024)S(1)}, f32[8192]{0:T(1024)}, u32[]{:S(2)}) copy-start(f32[8192]{0:T(1024)} %param.7) | copy-start | bytes 98308
  0.0 49.7 %copy-start = (f32[4,8192]{1,0:T(4,128)S(1)}, f32[4,8192]{1,0:T(4,128)}, u32[]{:S(2)}) copy-start(f32[4,8192]{1,0:T(4,128)} %kelvin_ref.1) | copy-start | bytes 393220
  0.9 1.5 %copy-start.2 = (s32[256]{0:T(256)}, s32[256]{0:T(256)S(1)}, u32[]{:S(2)}) copy-start(s32[256]{0:T(256)S(1)} %reshape.12.gather_ref) | copy-start | bytes 3076

commit v2 on v1

--- a/solution.py
+++ b/solution.py
@@ -33,12 +33,16 @@
     running,
     mix,
     stage,
+    keep,
+    mid_recv,
     adj_recv,
     tile_sem,
     em_send_sem,
     em_recv_sem,
     loss_send_sem,
     loss_recv_sem,
+    mid_send_sem,
+    mid_recv_sem,
     adj_send_sem,
     adj_recv_sem,
 ):
@@ -50,6 +54,12 @@
     chunks = blocks // CHUNK
     ch_rows = CHUNK * tl
     entries = rows * slots
+    depth = n // 2
+    line, y = me // 2, lax.rem(me, 2)
+    partner = line * 2 + 1 - y
+
+    def along(d):
+        return lax.rem(line + d + depth, depth) * 2
 
     def tile_copy(r):
         return pltpu.make_async_copy(tiles_hbm.at[r], tiles.at[r], tile_sem.at[r])
@@ -69,7 +79,7 @@
             cols = pl.ds(pl.multiple_of((ch * CHUNK + i) * side, side), side)
             t2 = kelvin_ref[:, cols] * kelvin_ref[:, cols]
             stage[i * tl : (i + 1) * tl, :] = emit_ref[pl.ds(ch * CHUNK + i, 1), :] * (t2 * t2)
-        em_recv[me, pl.ds(first, ch_rows), :] = stage[...].astype(BF16)
+        em_recv[me, ch] = stage[...].astype(BF16)
         for i in range(CHUNK):
             cols = pl.ds(pl.multiple_of((ch * CHUNK + i) * side, side), side)
             stage[i * tl : (i + 1) * tl, :] = loss_ref[:, cols]
@@ -100,8 +110,9 @@
             device_id_type=MESH,
         )
 
-    for o in range(1, n):
-        em_copy(o, me, lax.rem(me + o, n)).start()
+    for d in reversed(range(1, depth)):
+        em_copy(d, me, along(d) + y).start()
+    em_copy(0, me, partner).start()
     for o in range(1, n):
         loss_copy(o, me, lax.rem(me + o, n)).start()
 
@@ -111,13 +122,16 @@
     own_part = pl.multiple_of(me * (rows * tl), rows * tl)
     loss_recv[me] = loss_send[pl.ds(own_part, rows * tl), :]
 
-    for o in range(1, n):
-        em_copy(o, lax.rem(me + n - o, n), lax.rem(me + o, n)).wait()
+    for d in range(1, depth):
+        em_copy(d, along(-d) + y, along(d) + y).wait()
+        em_copy(depth + d, along(-d) + y, partner).start()
+    em_copy(0, partner, partner).wait()
+    for d in range(1, depth):
+        em_copy(depth + d, along(-d) + 1 - y, partner).wait()
 
     def em_chunk(ch, carry):
-        first = pl.multiple_of(ch * ch_rows, ch_rows)
         for s in range(n):
-            mix[pl.ds(s, ch_rows, stride=n), :] = em_recv[s, pl.ds(first, ch_rows), :].astype(F32)
+            mix[pl.ds(s, ch_rows, stride=n), :] = em_recv[s, ch].astype(F32)
         for i in range(CHUNK):
             em[ch * CHUNK + i] = mix[i * samples : (i + 1) * samples, :].astype(BF16)
         return carry
@@ -133,10 +147,12 @@
 
     def row_step(r, carry):
         flux = jnp.zeros((samples, side), F32)
-        for k in range(slots):
+        for k in range(0, slots, 2):
             flux += lax.dot_general(
-                em[gather_ref[r * slots + k]],
-                tiles[r, k],
+                jnp.concatenate(
+                    [em[gather_ref[r * slots + k]], em[gather_ref[r * slots + k + 1]]], axis=1
+                ),
+                jnp.concatenate([tiles[r, k], tiles[r, k + 1]], axis=1),
                 (((1,), (1,)), ((), ())),
                 preferred_element_type=F32,
             )
@@ -145,46 +161,71 @@
         weight = here * (flux - own)
         neg_weight[r] = -weight
         weight_b = weight.astype(BF16)
-        for k in range(slots):
-            contrib = jnp.dot(weight_b, tiles[r, k], preferred_element_type=F32)
-            running[r * slots + k] = contrib + running[prev_ref[r * slots + k]]
+        for k in range(0, slots, 2):
+            pair = jnp.concatenate([tiles[r, k], tiles[r, k + 1]], axis=1)
+            contrib = jnp.dot(weight_b, pair, preferred_element_type=F32)
+            for e in range(2):
+                at = r * slots + k + e
+                running[at] = contrib[:, e * side : (e + 1) * side] + running[prev_ref[at]]
         return carry
 
     lax.fori_loop(0, rows, row_step, 0)
 
-    def adj_copy(o, ch, src, dst):
-        first = pl.multiple_of(ch * ch_rows, ch_rows)
+    def mid_copy(ch):
         return pltpu.make_async_remote_copy(
-            src_ref=em_recv.at[dst, pl.ds(first, ch_rows)],
-            dst_ref=adj_recv.at[src, pl.ds(first, ch_rows)],
-            send_sem=adj_send_sem.at[o, ch],
-            recv_sem=adj_recv_sem.at[o, ch],
-            device_id={"node": dst},
+            src_ref=em_recv.at[pl.ds(0, depth), ch],
+            dst_ref=mid_recv.at[pl.ds(0, depth), ch],
+            send_sem=mid_send_sem.at[ch],
+            recv_sem=mid_recv_sem.at[ch],
+            device_id={"node": partner},
             device_id_type=MESH,
         )
 
-    def send_chunk(ch, carry):
-        first = pl.multiple_of(ch * ch_rows, ch_rows)
+    def adj_copy(d, ch):
+        return pltpu.make_async_remote_copy(
+            src_ref=em_recv.at[depth + d, ch],
+            dst_ref=adj_recv.at[d, ch],
+            send_sem=adj_send_sem.at[d, ch],
+            recv_sem=adj_recv_sem.at[d, ch],
+            device_id={"node": along(d) + y},
+            device_id_type=MESH,
+        )
+
+    def split_chunk(ch):
         for i in range(CHUNK):
             c = ch * CHUNK + i
             off = c - me * rows
             mine = jnp.where((off >= 0) & (off < rows), off, rows)
             mix[i * samples : (i + 1) * samples, :] = running[last_ref[c]] + neg_weight[mine]
-        for s in range(n):
-            em_recv[s, pl.ds(first, ch_rows), :] = mix[pl.ds(s, ch_rows, stride=n), :].astype(BF16)
-        for o in range(1, n):
-            adj_copy(o, ch, me, lax.rem(me + o, n)).start()
-        return carry
-
-    lax.fori_loop(0, chunks, send_chunk, 0)
+        for z in range(depth):
+            other = mix[pl.ds(2 * z + 1 - y, ch_rows, stride=n), :]
+            em_recv[z, ch] = other.astype(BF16)
+        mid_copy(ch).start()
+        for z in range(depth):
+            keep[z, ch] = mix[pl.ds(2 * z + y, ch_rows, stride=n), :]
+
+    def pass_chunk(ch):
+        mid_copy(ch).wait()
+        for d in reversed(range(1, depth)):
+            z = lax.rem(line + d, depth)
+            em_recv[depth + d, ch] = (keep[z, ch] + mid_recv[z, ch].astype(F32)).astype(BF16)
+            adj_copy(d, ch).start()
+
+    split_chunk(0)
+
+    def send_step(ch, carry):
+        split_chunk(ch)
+        pass_chunk(ch - 1)
+        return carry
+
+    lax.fori_loop(1, chunks, send_step, 0)
+    pass_chunk(chunks - 1)
 
     def sum_chunk(ch, carry):
-        first = pl.multiple_of(ch * ch_rows, ch_rows)
-        total = em_recv[me, pl.ds(first, ch_rows), :].astype(F32)
-        for o in range(1, n):
-            src = lax.rem(me + n - o, n)
-            adj_copy(o, ch, src, lax.rem(me + o, n)).wait()
-            total += adj_recv[src, pl.ds(first, ch_rows), :].astype(F32)
+        total = keep[line, ch] + mid_recv[line, ch].astype(F32)
+        for d in range(1, depth):
+            adj_copy(d, ch).wait()
+            total += adj_recv[d, ch].astype(F32)
         stage[...] = total
         for i in range(CHUNK):
             cols = pl.ds(pl.multiple_of((ch * CHUNK + i) * side, side), side)
@@ -208,6 +249,7 @@
     blocks = surfaces // side
     samples = tl * n
     entries = rows * slots
+    chunked = (blocks // CHUNK, CHUNK * tl, side)
 
     in_use = jnp.arange(slots, dtype=jnp.int32)[None, :] < tile_slots_occupied[:, None]
     target = jnp.where(in_use, tile_target_index, blocks).reshape(entries)
@@ -228,7 +270,7 @@
         out_specs=vmem,
         scratch_shapes=[
             pltpu.VMEM(gebhart_tiles.shape, BF16),
-            pltpu.VMEM((n, blocks * tl, side), BF16),
+            pltpu.VMEM((n,) + chunked, BF16),
             pltpu.VMEM((blocks + 1, samples, side), BF16),
             pltpu.VMEM((blocks * tl, side), BF16),
             pltpu.VMEM((n, rows * tl, side), BF16),
@@ -237,17 +279,21 @@
             pltpu.VMEM((entries + 1, samples, side), F32),
             pltpu.VMEM((CHUNK * samples, side), F32),
             pltpu.VMEM((CHUNK * tl, side), F32),
-            pltpu.VMEM((n, blocks * tl, side), BF16),
+            pltpu.VMEM((n // 2,) + chunked, F32),
+            pltpu.VMEM((n // 2,) + chunked, BF16),
+            pltpu.VMEM((n // 2,) + chunked, BF16),
             pltpu.SemaphoreType.DMA((rows,)),
             pltpu.SemaphoreType.DMA((n,)),
             pltpu.SemaphoreType.DMA((n,)),
             pltpu.SemaphoreType.DMA((n,)),
             pltpu.SemaphoreType.DMA((n,)),
-            pltpu.SemaphoreType.DMA((n, blocks // CHUNK)),
-            pltpu.SemaphoreType.DMA((n, blocks // CHUNK)),
+            pltpu.SemaphoreType.DMA((blocks // CHUNK,)),
+            pltpu.SemaphoreType.DMA((blocks // CHUNK,)),
+            pltpu.SemaphoreType.DMA((n // 2, blocks // CHUNK)),
+            pltpu.SemaphoreType.DMA((n // 2, blocks // CHUNK)),
         ],
         compiler_params=pltpu.CompilerParams(
-            collective_id=0, has_side_effects=True, vmem_limit_bytes=60 * 2**20
+            collective_id=0, has_side_effects=True, vmem_limit_bytes=62 * 2**20
         ),
     )(
         scaled_kelvin,

time: 51.4 us -> 44 us (0.86)
  Pallas kernels: 47.3 us -> 39.9 us
    pallas_call x1, Pallas kernels: 47.3 us -> 39.9 us  [on_device(): pl.pallas_call(functools.partial(kernel, n), out_shape=jax.ShapeDtypeStru...]
where the time goes in v2:
time: 44 us; the launch traced here: 43.9 us
  Pallas kernels  39.9 us (91%)
  other arithmetic  3.88 us (9%)
    pallas_call x1, Pallas kernels, on_device(): pl.pallas_call(functools.partial(kernel, n), out_shape=jax.ShapeDtypeStru...  39.9 us
    mul x2, other arithmetic, on_device(): return 4.0 * surface_emittance[None, :] * scaled_kelvin ** 3 * adjoint  1.62 us

profile of v2, /device:TPU:0, one launch (start us, length us, event | category | flops | bytes accessed | tf_op | source)
XLA Modules:
  0.0 43.9 jit_solution(13439700429165180583)
XLA Ops:
  0.0 0.0 copy-start.1
  0.0 0.0 copy-start
  0.0 0.8 %fusion.3 = s32[8,32]{1,0:T(8,128)S(1)} fusion(s32[8,32]{1,0:T(8,128)} %param.10, s32[8]{0:T(128)} %param.11), kind=kLoop, calls=%fused_computation.10 | loop fusion | flops 512 | bytes 2080 | tf_op jit(solution)/shard_map/jit(_where)/select_n | solution.py:255
  0.8 0.1 reshape.12.gather_ref
  0.9 0.0 copy-start.2
  0.9 0.2 select_reduce_fusion
  1.1 0.6 %compare_select_fusion.prev_ref = s32[256]{0:T(256)} fusion(s32[256]{0:T(256)S(1)} %select_reduce_fusion), kind=kLoop, calls=%fused_computation.11 | loop fusion | flops 512 | bytes 2048 | tf_op jit(solution)/shard_map/jit(_where)/select_n | solution.py:259
  1.6 0.1 select_reduce_fusion.1
  1.8 0.6 %compare_select_fusion.1.last_ref = s32[64]{0:T(128)} fusion(s32[64]{0:T(128)S(1)} %select_reduce_fusion.1), kind=kLoop, calls=%fused_computation.12 | loop fusion | flops 128 | bytes 512 | tf_op jit(solution)/shard_map/jit(_where)/select_n | solution.py:262
  2.4 0.0 copy-done.2
  2.4 39.9 %shard_map.64 = f32[4,8192]{1,0:T(4,128)} custom-call(f32[4,8192]{1,0:T(4,128)} %kelvin_ref.1, f32[64,128]{1,0:T(8,128)} %bitcast.1, f32[4,8192]{1,0:T(4,128)} %loss_ref.1, bf16[8,32,128,128]{3,2,1,0:T(8,128)(2,1)} %tiles_hbm.1, s32[256]{0:T(256)} %copy-done.2, s32[256]{0:T(256)} %compare_select_fusion.prev_ref, s32[64]{0:T(128)} %compare_select_fusion.1.last_ref), custom_call_target="tpu_custom_call" | custom-call | tf_op jit(solution)/shard_map/pallas_call | solution.py:266
  42.2 0.0 copy-done.1
  42.3 0.0 copy-done
  42.3 1.6 %fusion.2 = f32[4,8192]{1,0:T(4,128)} fusion(f32[4,8192]{1,0:T(4,128)} %shard_map.64, f32[4,8192]{1,0:T(4,128)S(1)} %copy-done, f32[8192]{0:T(1024)S(1)} %broadcast_multiply_fusion), kind=kLoop, calls=%fused_computation.5 | loop fusion | flops 131072 | bytes 425984 | tf_op jit(solution)/shard_map/mul | solution.py:307
  (1 shorter events, 0.0 us)
Async XLA Ops:
  0.0 42.2 %copy-start.1 = (f32[8192]{0:T(1024)S(1)}, f32[8192]{0:T(1024)}, u32[]{:S(2)}) copy-start(f32[8192]{0:T(1024)} %param.7) | copy-start | bytes 98308
  0.0 42.3 %copy-start = (f32[4,8192]{1,0:T(4,128)S(1)}, f32[4,8192]{1,0:T(4,128)}, u32[]{:S(2)}) copy-start(f32[4,8192]{1,0:T(4,128)} %kelvin_ref.1) | copy-start | bytes 393220
  0.9 1.5 %copy-start.2 = (s32[256]{0:T(256)}, s32[256]{0:T(256)S(1)}, u32[]{:S(2)}) copy-start(s32[256]{0:T(256)S(1)} %reshape.12.gather_ref) | copy-start | bytes 3076

commit v3 on v2

--- a/solution.py
+++ b/solution.py
@@ -20,8 +20,7 @@
     loss_ref,
     tiles_hbm,
     gather_ref,
-    prev_ref,
-    last_ref,
+    chain_ref,
     out_ref,
     tiles,
     em_recv,
@@ -30,6 +29,7 @@
     loss_recv,
     loss_rows,
     neg_weight,
+    weight_b,
     running,
     mix,
     stage,
@@ -73,28 +73,27 @@
             barrier, inc=1, device_id={"node": lax.rem(me + o, n)}, device_id_type=MESH
         )
 
-    def emit_chunk(ch, carry):
-        first = pl.multiple_of(ch * ch_rows, ch_rows)
+    def emit_chunk(ch):
         for i in range(CHUNK):
             cols = pl.ds(pl.multiple_of((ch * CHUNK + i) * side, side), side)
             t2 = kelvin_ref[:, cols] * kelvin_ref[:, cols]
             stage[i * tl : (i + 1) * tl, :] = emit_ref[pl.ds(ch * CHUNK + i, 1), :] * (t2 * t2)
         em_recv[me, ch] = stage[...].astype(BF16)
+
+    def loss_chunk(ch, carry):
         for i in range(CHUNK):
             cols = pl.ds(pl.multiple_of((ch * CHUNK + i) * side, side), side)
             stage[i * tl : (i + 1) * tl, :] = loss_ref[:, cols]
+        first = pl.multiple_of(ch * ch_rows, ch_rows)
         loss_send[pl.ds(first, ch_rows), :] = stage[...].astype(BF16)
         return carry
 
-    lax.fori_loop(0, chunks, emit_chunk, 0)
-    pl.semaphore_wait(barrier, n - 1)
-
-    def em_copy(o, src, dst):
+    def em_copy(o, ch, src, dst):
         return pltpu.make_async_remote_copy(
-            src_ref=em_recv.at[src],
-            dst_ref=em_recv.at[src],
-            send_sem=em_send_sem.at[o],
-            recv_sem=em_recv_sem.at[o],
+            src_ref=em_recv.at[src, ch],
+            dst_ref=em_recv.at[src, ch],
+            send_sem=em_send_sem.at[o, ch],
+            recv_sem=em_recv_sem.at[o, ch],
             device_id={"node": dst},
             device_id_type=MESH,
         )
@@ -110,33 +109,54 @@
             device_id_type=MESH,
         )
 
-    for d in reversed(range(1, depth)):
-        em_copy(d, me, along(d) + y).start()
-    em_copy(0, me, partner).start()
+    def em_start(ch):
+        for d in reversed(range(1, depth)):
+            em_copy(d, ch, me, along(d) + y).start()
+        em_copy(0, ch, me, partner).start()
+
+    emit_chunk(0)
+    pl.semaphore_wait(barrier, n - 1)
+    em_start(0)
+
+    def emit_step(ch, carry):
+        emit_chunk(ch)
+        em_start(ch)
+        return carry
+
+    lax.fori_loop(1, chunks, emit_step, 0)
+    lax.fori_loop(0, chunks, loss_chunk, 0)
     for o in range(1, n):
         loss_copy(o, me, lax.rem(me + o, n)).start()
 
     em[blocks] = jnp.zeros((samples, side), BF16)
     neg_weight[rows] = jnp.zeros((samples, side), F32)
-    running[entries] = jnp.zeros((samples, side), F32)
+    running[0] = jnp.zeros((samples, side), F32)
     own_part = pl.multiple_of(me * (rows * tl), rows * tl)
     loss_recv[me] = loss_send[pl.ds(own_part, rows * tl), :]
 
-    for d in range(1, depth):
-        em_copy(d, along(-d) + y, along(d) + y).wait()
-        em_copy(depth + d, along(-d) + y, partner).start()
-    em_copy(0, partner, partner).wait()
-    for d in range(1, depth):
-        em_copy(depth + d, along(-d) + 1 - y, partner).wait()
-
-    def em_chunk(ch, carry):
+    def forward_chunk(ch):
+        for d in range(1, depth):
+            em_copy(d, ch, along(-d) + y, along(d) + y).wait()
+            em_copy(depth + d, ch, along(-d) + y, partner).start()
+
+    def em_chunk(ch):
+        em_copy(0, ch, partner, partner).wait()
+        for d in range(1, depth):
+            em_copy(depth + d, ch, along(-d) + 1 - y, partner).wait()
         for s in range(n):
             mix[pl.ds(s, ch_rows, stride=n), :] = em_recv[s, ch].astype(F32)
         for i in range(CHUNK):
             em[ch * CHUNK + i] = mix[i * samples : (i + 1) * samples, :].astype(BF16)
-        return carry
-
-    lax.fori_loop(0, chunks, em_chunk, 0)
+
+    forward_chunk(0)
+
+    def gather_step(ch, carry):
+        forward_chunk(ch)
+        em_chunk(ch - 1)
+        return carry
+
+    lax.fori_loop(1, chunks, gather_step, 0)
+    em_chunk(chunks - 1)
 
     for o in range(1, n):
         loss_copy(o, lax.rem(me + n - o, n), lax.rem(me + o, n)).wait()
@@ -145,7 +165,7 @@
     for r in range(rows):
         tile_copy(r).wait()
 
-    def row_step(r, carry):
+    def ahead(r):
         flux = jnp.zeros((samples, side), F32)
         for k in range(0, slots, 2):
             flux += lax.dot_general(
@@ -160,16 +180,25 @@
         here = loss_rows[pl.ds(pl.multiple_of(r * samples, samples), samples), :]
         weight = here * (flux - own)
         neg_weight[r] = -weight
-        weight_b = weight.astype(BF16)
+        weight_b[r] = weight.astype(BF16)
+
+    def back(r):
         for k in range(0, slots, 2):
             pair = jnp.concatenate([tiles[r, k], tiles[r, k + 1]], axis=1)
-            contrib = jnp.dot(weight_b, pair, preferred_element_type=F32)
+            contrib = jnp.dot(weight_b[r], pair, preferred_element_type=F32)
             for e in range(2):
                 at = r * slots + k + e
-                running[at] = contrib[:, e * side : (e + 1) * side] + running[prev_ref[at]]
-        return carry
-
-    lax.fori_loop(0, rows, row_step, 0)
+                running[at + 1] = contrib[:, e * side : (e + 1) * side] + running[chain_ref[at]]
+
+    ahead(0)
+
+    def row_step(r, carry):
+        back(r - 1)
+        ahead(r)
+        return carry
+
+    lax.fori_loop(1, rows, row_step, 0)
+    back(rows - 1)
 
     def mid_copy(ch):
         return pltpu.make_async_remote_copy(
@@ -196,7 +225,7 @@
             c = ch * CHUNK + i
             off = c - me * rows
             mine = jnp.where((off >= 0) & (off < rows), off, rows)
-            mix[i * samples : (i + 1) * samples, :] = running[last_ref[c]] + neg_weight[mine]
+            mix[i * samples : (i + 1) * samples, :] = running[chain_ref[entries + c]] + neg_weight[mine]
         for z in range(depth):
             other = mix[pl.ds(2 * z + 1 - y, ch_rows, stride=n), :]
             em_recv[z, ch] = other.astype(BF16)
@@ -229,7 +258,9 @@
         stage[...] = total
         for i in range(CHUNK):
             cols = pl.ds(pl.multiple_of((ch * CHUNK + i) * side, side), side)
-            out_ref[:, cols] = stage[i * tl : (i + 1) * tl, :]
+            t1 = kelvin_ref[:, cols]
+            scale = 4.0 * emit_ref[pl.ds(ch * CHUNK + i, 1), :] * (t1 * t1 * t1)
+            out_ref[:, cols] = scale * stage[i * tl : (i + 1) * tl, :]
         return carry
 
     lax.fori_loop(0, chunks, sum_chunk, 0)
@@ -254,19 +285,17 @@
     in_use = jnp.arange(slots, dtype=jnp.int32)[None, :] < tile_slots_occupied[:, None]
     target = jnp.where(in_use, tile_target_index, blocks).reshape(entries)
     at = jnp.arange(entries, dtype=jnp.int32)
-    same = (target[:, None] == target[None, :]) & (at[None, :] < at[:, None])
-    prev = jnp.max(jnp.where(same, at[None, :], -1), axis=1)
-    prev = jnp.where(prev < 0, entries, prev)
-    hit = jnp.arange(blocks, dtype=jnp.int32)[:, None] == target[None, :]
-    last = jnp.max(jnp.where(hit, at[None, :], -1), axis=1)
-    last = jnp.where(last < 0, entries, last)
+    column = jnp.concatenate([target, jnp.arange(blocks, dtype=jnp.int32)])
+    limit = jnp.minimum(jnp.arange(entries + blocks, dtype=jnp.int32), entries)
+    same = (column[:, None] == target[None, :]) & (at[None, :] < limit[:, None])
+    chain = jnp.max(jnp.where(same, at[None, :] + 1, 0), axis=1)
 
     vmem = pl.BlockSpec(memory_space=pltpu.VMEM)
     smem = pl.BlockSpec(memory_space=pltpu.SMEM)
-    adjoint = pl.pallas_call(
+    return pl.pallas_call(
         functools.partial(kernel, n),
         out_shape=jax.ShapeDtypeStruct((tl, surfaces), F32),
-        in_specs=[vmem, vmem, vmem, pl.BlockSpec(memory_space=pl.ANY), smem, smem, smem],
+        in_specs=[vmem, vmem, vmem, pl.BlockSpec(memory_space=pl.ANY), smem, smem],
         out_specs=vmem,
         scratch_shapes=[
             pltpu.VMEM(gebhart_tiles.shape, BF16),
@@ -276,6 +305,7 @@
             pltpu.VMEM((n, rows * tl, side), BF16),
             pltpu.VMEM((rows * samples, side), F32),
             pltpu.VMEM((rows + 1, samples, side), F32),
+            pltpu.VMEM((rows, samples, side), BF16),
             pltpu.VMEM((entries + 1, samples, side), F32),
             pltpu.VMEM((CHUNK * samples, side), F32),
             pltpu.VMEM((CHUNK * tl, side), F32),
@@ -283,8 +313,8 @@
             pltpu.VMEM((n // 2,) + chunked, BF16),
             pltpu.VMEM((n // 2,) + chunked, BF16),
             pltpu.SemaphoreType.DMA((rows,)),
-            pltpu.SemaphoreType.DMA((n,)),
-            pltpu.SemaphoreType.DMA((n,)),
+            pltpu.SemaphoreType.DMA((n, blocks // CHUNK)),
+            pltpu.SemaphoreType.DMA((n, blocks // CHUNK)),
             pltpu.SemaphoreType.DMA((n,)),
             pltpu.SemaphoreType.DMA((n,)),
             pltpu.SemaphoreType.DMA((blocks // CHUNK,)),
@@ -301,10 +331,8 @@
         loss_factors,
         gebhart_tiles,
         target,
-        prev,
-        last,
+        chain,
     )
-    return 4.0 * surface_emittance[None, :] * scaled_kelvin**3 * adjoint
 
 
 def solution(mesh):

time: 44 us -> 41.1 us (0.934)
  Pallas kernels: 39.9 us -> 37.6 us
  other arithmetic: 3.88 us -> 1.59 us
  local copies, waits for them, and re-layouts: 0.09 us -> 1.65 us
    pallas_call x1, Pallas kernels: 39.9 us -> 37.6 us  [on_device(): pl.pallas_call(functools.partial(kernel, n), out_shape=jax.ShapeDtypeStru...]
    mul x2 -> x0, other arithmetic: 1.62 us -> none  [on_device(): return 4.0 * surface_emittance[None, :] * scaled_kelvin ** 3 * adjoint]
    unnamed x6 -> x3, local copies, waits for them, and re-layouts: 0.01 us -> 1.57 us
    select_n x2 -> x0, other arithmetic: 1.17 us -> none  [the longest x1 0.59 us: on_device(): last = jnp.where(last < 0, entries, last)]
    reduce_max x2 -> x1, other arithmetic: 0.29 us -> 0.83 us  [on_device(): chain = jnp.max(jnp.where(same, at[None, :] + 1, 0), axis=1)]
where the time goes in v3:
time: 41.1 us; the launch traced here: 40.9 us
  Pallas kernels  37.6 us (91%)
  local copies, waits for them, and re-layouts  1.65 us (4%)
  other arithmetic  1.59 us (4%)
    pallas_call x1, Pallas kernels, on_device(): pl.pallas_call(functools.partial(kernel, n), out_shape=jax.ShapeDtypeStru...  37.6 us
    unnamed x3, local copies, waits for them, and re-layouts  1.57 us
    reduce_max x1, other arithmetic, on_device(): chain = jnp.max(jnp.where(same, at[None, :] + 1, 0), axis=1)  0.83 us

profile of v3, /device:TPU:0, one launch (start us, length us, event | category | flops | bytes accessed | tf_op | source)
XLA Modules:
  0.0 40.9 jit_solution(7528238483830479329)
XLA Ops:
  0.0 0.8 %fusion.1 = s32[8,32]{1,0:T(8,128)S(1)} fusion(s32[8,32]{1,0:T(8,128)} %param.10, s32[8]{0:T(128)} %param.11), kind=kLoop, calls=%fused_computation.4 | loop fusion | flops 512 | bytes 2080 | tf_op jit(solution)/shard_map/jit(_where)/select_n | solution.py:286
  0.8 0.1 reshape.19.gather_ref
  0.8 0.0 copy-start
  0.9 0.8 %select_reduce_fusion.chain_ref = s32[320]{0:T(512)} fusion(s32[256]{0:T(256)S(1)} %iota_add_fusion, s32[320]{0:T(512)S(1)} %get-tuple-element.6, s32[256]{0:T(256)S(1)} %reshape.19.gather_ref, s32[320]{0:T(512)S(1)} %get-tuple-element.5), kind=kLoop, calls=%fused_computation | loop fusion | flops 409280 | bytes 5888 | tf_op jit(solution)/shard_map/reduce_max | solution.py:291
  1.7 0.0 copy-done
  1.7 37.6 %shard_map.64 = f32[4,8192]{1,0:T(4,128)} custom-call(f32[4,8192]{1,0:T(4,128)} %kelvin_ref.1, f32[64,128]{1,0:T(8,128)} %bitcast.1, f32[4,8192]{1,0:T(4,128)} %loss_ref.1, bf16[8,32,128,128]{3,2,1,0:T(8,128)(2,1)} %tiles_hbm.1, s32[256]{0:T(256)} %copy-done, s32[320]{0:T(512)} %select_reduce_fusion.chain_ref), custom_call_target="tpu_custom_call" | custom-call | tf_op jit(solution)/shard_map/pallas_call | solution.py:295
  39.3 1.6 %copy.8 = f32[4,8192]{1,0:T(4,128)} copy(f32[4,8192]{1,0:T(4,128)} %shard_map.64) | data formatting | bytes 262144
  (3 shorter events, 0.0 us)
Async XLA Ops:
  0.8 0.8 %copy-start = (s32[256]{0:T(256)}, s32[256]{0:T(256)S(1)}, u32[]{:S(2)}) copy-start(s32[256]{0:T(256)S(1)} %reshape.19.gather_ref) | copy-start | bytes 3076

commit v4 on v3

--- a/solution.py
+++ b/solution.py
@@ -10,6 +10,7 @@
 MESH = pl.DeviceIdType.MESH
 F32 = jnp.float32
 BF16 = jnp.bfloat16
+LANES = 128
 CHUNK = 16
 
 
@@ -19,8 +20,9 @@
     emit_ref,
     loss_ref,
     tiles_hbm,
-    gather_ref,
-    chain_ref,
+    target_ref,
+    target_vec_ref,
+    used_ref,
     out_ref,
     tiles,
     em_recv,
@@ -30,6 +32,11 @@
     loss_rows,
     neg_weight,
     weight_b,
+    wide,
+    prev_vec,
+    last_vec,
+    prev_ref,
+    last_ref,
     running,
     mix,
     stage,
@@ -37,6 +44,7 @@
     mid_recv,
     adj_recv,
     tile_sem,
+    index_sem,
     em_send_sem,
     em_recv_sem,
     loss_send_sem,
@@ -61,6 +69,9 @@
     def along(d):
         return lax.rem(line + d + depth, depth) * 2
 
+    def column(r, k):
+        return jnp.where(k < used_ref[r], target_ref[r, k], blocks)
+
     def tile_copy(r):
         return pltpu.make_async_copy(tiles_hbm.at[r], tiles.at[r], tile_sem.at[r])
 
@@ -134,6 +145,36 @@
     own_part = pl.multiple_of(me * (rows * tl), rows * tl)
     loss_recv[me] = loss_send[pl.ds(own_part, rows * tl), :]
 
+    lane = lax.broadcasted_iota(jnp.int32, wide.shape, 1)
+    row = lax.broadcasted_iota(jnp.int32, wide.shape, 0)
+    wide[...] = jnp.full(wide.shape, blocks, jnp.int32)
+    wide[:, :slots] = target_vec_ref[...]
+    used = jnp.zeros(wide.shape, jnp.int32)
+    for r in range(rows):
+        used = jnp.where(row == r, used_ref[r], used)
+    columns = jnp.where(lane < used, wide[...], blocks)
+    place = row * slots + lane
+    spot = lax.broadcasted_iota(jnp.int32, last_vec.shape, 0) * LANES
+    spot += lax.broadcasted_iota(jnp.int32, last_vec.shape, 1)
+
+    def index_step(r, carry):
+        prev, last = carry
+        for k in range(slots):
+            at = r * slots + k
+            c = column(r, k)
+            prev = jnp.where((columns == c) & (place > at), at + 1, prev)
+            last = jnp.where(spot == c, at + 1, last)
+        return prev, last
+
+    none = (jnp.zeros(prev_vec.shape, jnp.int32), jnp.zeros(last_vec.shape, jnp.int32))
+    prev_vec[...], last_vec[...] = lax.fori_loop(0, rows, index_step, none)
+    index_copies = (
+        pltpu.make_async_copy(prev_vec, prev_ref, index_sem.at[0]),
+        pltpu.make_async_copy(last_vec, last_ref, index_sem.at[1]),
+    )
+    for copy in index_copies:
+        copy.start()
+
     def forward_chunk(ch):
         for d in range(1, depth):
             em_copy(d, ch, along(-d) + y, along(d) + y).wait()
@@ -170,7 +211,7 @@
         for k in range(0, slots, 2):
             flux += lax.dot_general(
                 jnp.concatenate(
-                    [em[gather_ref[r * slots + k]], em[gather_ref[r * slots + k + 1]]], axis=1
+                    [em[column(r, k)], em[column(r, k + 1)]], axis=1
                 ),
                 jnp.concatenate([tiles[r, k], tiles[r, k + 1]], axis=1),
                 (((1,), (1,)), ((), ())),
@@ -188,8 +229,10 @@
             contrib = jnp.dot(weight_b[r], pair, preferred_element_type=F32)
             for e in range(2):
                 at = r * slots + k + e
-                running[at + 1] = contrib[:, e * side : (e + 1) * side] + running[chain_ref[at]]
-
+                running[at + 1] = contrib[:, e * side : (e + 1) * side] + running[prev_ref[r, k + e]]
+
+    for copy in index_copies:
+        copy.wait()
     ahead(0)
 
     def row_step(r, carry):
@@ -225,7 +268,7 @@
             c = ch * CHUNK + i
             off = c - me * rows
             mine = jnp.where((off >= 0) & (off < rows), off, rows)
-            mix[i * samples : (i + 1) * samples, :] = running[chain_ref[entries + c]] + neg_weight[mine]
+            mix[i * samples : (i + 1) * samples, :] = running[last_ref[c // LANES, lax.rem(c, LANES)]] + neg_weight[mine]
         for z in range(depth):
             other = mix[pl.ds(2 * z + 1 - y, ch_rows, stride=n), :]
             em_recv[z, ch] = other.astype(BF16)
@@ -282,20 +325,12 @@
     entries = rows * slots
     chunked = (blocks // CHUNK, CHUNK * tl, side)
 
-    in_use = jnp.arange(slots, dtype=jnp.int32)[None, :] < tile_slots_occupied[:, None]
-    target = jnp.where(in_use, tile_target_index, blocks).reshape(entries)
-    at = jnp.arange(entries, dtype=jnp.int32)
-    column = jnp.concatenate([target, jnp.arange(blocks, dtype=jnp.int32)])
-    limit = jnp.minimum(jnp.arange(entries + blocks, dtype=jnp.int32), entries)
-    same = (column[:, None] == target[None, :]) & (at[None, :] < limit[:, None])
-    chain = jnp.max(jnp.where(same, at[None, :] + 1, 0), axis=1)
-
     vmem = pl.BlockSpec(memory_space=pltpu.VMEM)
     smem = pl.BlockSpec(memory_space=pltpu.SMEM)
     return pl.pallas_call(
         functools.partial(kernel, n),
         out_shape=jax.ShapeDtypeStruct((tl, surfaces), F32),
-        in_specs=[vmem, vmem, vmem, pl.BlockSpec(memory_space=pl.ANY), smem, smem],
+        in_specs=[vmem, vmem, vmem, pl.BlockSpec(memory_space=pl.ANY), smem, vmem, smem],
         out_specs=vmem,
         scratch_shapes=[
             pltpu.VMEM(gebhart_tiles.shape, BF16),
@@ -306,6 +341,11 @@
             pltpu.VMEM((rows * samples, side), F32),
             pltpu.VMEM((rows + 1, samples, side), F32),
             pltpu.VMEM((rows, samples, side), BF16),
+            pltpu.VMEM((rows, LANES), jnp.int32),
+            pltpu.VMEM((rows, LANES), jnp.int32),
+            pltpu.VMEM((8, LANES), jnp.int32),
+            pltpu.SMEM((rows, LANES), jnp.int32),
+            pltpu.SMEM((8, LANES), jnp.int32),
             pltpu.VMEM((entries + 1, samples, side), F32),
             pltpu.VMEM((CHUNK * samples, side), F32),
             pltpu.VMEM((CHUNK * tl, side), F32),
@@ -313,6 +353,7 @@
             pltpu.VMEM((n // 2,) + chunked, BF16),
             pltpu.VMEM((n // 2,) + chunked, BF16),
             pltpu.SemaphoreType.DMA((rows,)),
+            pltpu.SemaphoreType.DMA((2,)),
             pltpu.SemaphoreType.DMA((n, blocks // CHUNK)),
             pltpu.SemaphoreType.DMA((n, blocks // CHUNK)),
             pltpu.SemaphoreType.DMA((n,)),
@@ -330,8 +371,9 @@
         surface_emittance.reshape(blocks, side),
         loss_factors,
         gebhart_tiles,
-        target,
-        chain,
+        tile_target_index,
+        tile_target_index,
+        tile_slots_occupied,
     )
 
 

time: 41.1 us -> 39.5 us (0.961)
  other arithmetic: 1.59 us -> 0 us
    reduce_max x1 -> x0, other arithmetic: 0.83 us -> none  [on_device(): chain = jnp.max(jnp.where(same, at[None, :] + 1, 0), axis=1)]
    select_n x1 -> x0, other arithmetic: 0.76 us -> none  [on_device(): target = jnp.where(in_use, tile_target_index, blocks).reshape(entries)]
    unnamed x3 -> x1, local copies, waits for them, and re-layouts: 1.57 us -> 1.57 us
where the time goes in v4:
time: 39.5 us; the launch traced here: 39.4 us
  Pallas kernels  37.8 us (96%)
  local copies, waits for them, and re-layouts  1.57 us (4%)
    pallas_call x1, Pallas kernels, on_device(): pl.pallas_call(functools.partial(kernel, n), out_shape=jax.ShapeDtypeStru...  37.8 us
    unnamed x1, local copies, waits for them, and re-layouts  1.57 us

profile of v4, /device:TPU:0, one launch (start us, length us, event | category | flops | bytes accessed | tf_op | source)
XLA Modules:
  0.0 39.4 jit_solution(18124608927809921258)
XLA Ops:
  0.0 37.8 %shard_map.64 = f32[4,8192]{1,0:T(4,128)} custom-call(f32[4,8192]{1,0:T(4,128)} %kelvin_ref.1, f32[64,128]{1,0:T(8,128)} %bitcast.1, f32[4,8192]{1,0:T(4,128)} %loss_ref.1, bf16[8,32,128,128]{3,2,1,0:T(8,128)(2,1)} %tiles_hbm.1, s32[8,32]{1,0:T(8,128)} %target_vec_ref.1, s32[8,32]{1,0:T(8,128)} %target_vec_ref.1, s32[8]{0:T(128)} %used_ref.1), custom_call_target="tpu_custom_call" | custom-call | tf_op jit(solution)/shard_map/pallas_call | solution.py:330
  37.8 1.6 %copy.8 = f32[4,8192]{1,0:T(4,128)} copy(f32[4,8192]{1,0:T(4,128)} %shard_map.64) | data formatting | bytes 262144

commit v5 on v4

--- a/solution.py
+++ b/solution.py
@@ -207,16 +207,15 @@
         tile_copy(r).wait()
 
     def ahead(r):
-        flux = jnp.zeros((samples, side), F32)
+        turned = jnp.zeros((side, samples), F32)
         for k in range(0, slots, 2):
-            flux += lax.dot_general(
-                jnp.concatenate(
-                    [em[column(r, k)], em[column(r, k + 1)]], axis=1
-                ),
+            turned += lax.dot_general(
                 jnp.concatenate([tiles[r, k], tiles[r, k + 1]], axis=1),
+                jnp.concatenate([em[column(r, k)], em[column(r, k + 1)]], axis=1),
                 (((1,), (1,)), ((), ())),
                 preferred_element_type=F32,
             )
+        flux = turned.T
         own = em[me * rows + r].astype(F32)
         here = loss_rows[pl.ds(pl.multiple_of(r * samples, samples), samples), :]
         weight = here * (flux - own)
@@ -329,7 +328,7 @@
     smem = pl.BlockSpec(memory_space=pltpu.SMEM)
     return pl.pallas_call(
         functools.partial(kernel, n),
-        out_shape=jax.ShapeDtypeStruct((tl, surfaces), F32),
+        out_shape=pltpu.VMEM((tl, surfaces), F32),
         in_specs=[vmem, vmem, vmem, pl.BlockSpec(memory_space=pl.ANY), smem, vmem, smem],
         out_specs=vmem,
         scratch_shapes=[

time: 39.5 us -> 38 us (0.962)
  local copies, waits for them, and re-layouts: 1.57 us -> 0.66 us
  Pallas kernels: 37.8 us -> 37.1 us
    unnamed x1, local copies, waits for them, and re-layouts: 1.57 us -> 0.66 us
    pallas_call x1, Pallas kernels: 37.8 us -> 37.1 us  [on_device(): pl.pallas_call(functools.partial(kernel, n), out_shape=pltpu.VMEM((tl, su...]
where the time goes in v5:
time: 38 us; the launch traced here: 37.8 us
  Pallas kernels  37.1 us (98%)
  local copies, waits for them, and re-layouts  0.66 us (2%)
    pallas_call x1, Pallas kernels, on_device(): pl.pallas_call(functools.partial(kernel, n), out_shape=pltpu.VMEM((tl, su...  37.1 us

profile of v5, /device:TPU:0, one launch (start us, length us, event | category | flops | bytes accessed | tf_op | source)
XLA Modules:
  0.0 37.8 jit_solution(6666760066625753053)
XLA Ops:
  0.0 37.1 %shard_map.64 = f32[4,8192]{1,0:T(4,128)S(1)} custom-call(f32[4,8192]{1,0:T(4,128)} %kelvin_ref.1, f32[64,128]{1,0:T(8,128)} %bitcast.1, f32[4,8192]{1,0:T(4,128)} %loss_ref.1, bf16[8,32,128,128]{3,2,1,0:T(8,128)(2,1)} %tiles_hbm.1, s32[8,32]{1,0:T(8,128)} %target_vec_ref.1, s32[8,32]{1,0:T(8,128)} %target_vec_ref.1, s32[8]{0:T(128)} %used_ref.1), custom_call_target="tpu_custom_call" | custom-call | tf_op jit(solution)/shard_map/pallas_call | solution.py:329
  37.1 0.7 %copy.8 = f32[4,8192]{1,0:T(4,128)} copy(f32[4,8192]{1,0:T(4,128)S(1)} %shard_map.64) | data formatting | bytes 262144
